TPU v7x, 256 devices: a whole 4x4x8 slice. The times are simulated.
256 devices in a mesh: req: 32 (over y, x, core), samp: 8 (over z).
Axes of the slice: x: 4, y: 4, z: 8, core: 2. Of those that a mesh axis runs over, the one named last changes fastest.
Arguments:
- features: bfloat16 [49152, 7168], P('req', 'samp'), may hold values from -6 to 6
- gate_input: bfloat16 [49152, 7168], P('req', 'samp'), may hold values from -15.5 to 15.5
- input_map: bfloat16 [49152, 128], P('req'), may hold values from -6 to 6
- output_map: bfloat16 [49152, 128], P('req'), may hold values from -6 to 6
- head_step_sizes: float32 [112, 49152], P('samp', 'req'), may hold values from 0.0005 to 0.6, as said below
- log_rate: float32 [112], P('samp'), may hold values from -0.35 to 0.35
- skip_gain: float32 [112], P('samp'), may hold values from 0.5 to 1.5
- norm_gain: float32 [7168], P('samp'), may hold values from 0.5 to 1.5
- cache_states: bfloat16 [512, 112, 4096], P('req', 'samp'), may hold values from -3 to 3
- hit_owner: int32 [512, 1], P('req'), may hold values from 0 to 31; in each aligned block of 16 rows (0 to 15, 16 to 31, ...) at most 2 rows name the same one
- hit_slot: int32 [512], P('req'), may hold values from 0 to 15
- suffix_blocks: int32 [32, 16], P('req'), may hold values from 1 to 4, 24 in all within a row
- dec_features: bfloat16 [512, 8, 2, 7168], P('req', None, None, 'samp'), may hold values from -6 to 6
- dec_gate: bfloat16 [512, 8, 2, 7168], P('req', None, None, 'samp'), may hold values from -15.5 to 15.5
- dec_input_map: bfloat16 [512, 8, 2, 128], P('req'), may hold values from -6 to 6
- dec_output_map: bfloat16 [512, 8, 2, 128], P('req'), may hold values from -6 to 6
- dec_step_size: float32 [112, 512, 8, 2], P('samp', 'req'), may hold values from 0.0005 to 0.6, as said below
Outputs:
- prefill_out: bfloat16 [49152, 7168], P('req', 'samp')
- decode_out: bfloat16 [512, 8, 2, 7168], P('req', None, None, 'samp')
Inputs may be any that keep to these rules, and one draw needn't show every extreme that they name: `hit_owner`: among the 16 requests of one device, at most 2 name the same owner, and some owner is named by 2 of them. `suffix_blocks`: each row sums to 24. `head_step_sizes`: Positive. `dec_step_size`: Positive.
All inputs are finite; a program needn't handle non-finite values.
Results may differ from a plain program's by a relative error of at most 0.0034.
Values may be sent and summed in bfloat16 or wider, within the bound.
No kernel may reach another device: no remote copies, remote signals or barrier semaphores. Data moves between devices by JAX's collectives and lax.ppermute only.
A program may use at most 192 MiB of HBM per device.

v0:
```python
import jax
import jax.numpy as jnp
from jax import lax
from jax.sharding import PartitionSpec as P

HEADS = 112
HEAD_DIM = 64
STATE = 64
GROUPS = 2
BLOCK_LEN = 64
CAP = 2
STEPS = 2
D_INNER = 7168


HIGH = lax.Precision.HIGHEST


def owner_ranks(owners):
    count = owners.shape[-1]
    same = owners[..., :, None] == owners[..., None, :]
    rows = lax.broadcasted_iota(jnp.int32, (count, count), 0)
    cols = lax.broadcasted_iota(jnp.int32, (count, count), 1)
    return jnp.sum(jnp.where(same & (cols < rows), 1, 0), axis=-1).astype(jnp.int32)


def slot_table(owners, ranks, places, owner_count):
    wanted = owners * CAP + ranks
    grid = lax.broadcasted_iota(jnp.int32, (1, owner_count * CAP), 1)
    table = jnp.sum(jnp.where(wanted[:, None] == grid, places[:, None], 0), axis=0)
    return table.reshape(owner_count, CAP)


def prefill(xval, bval, cval, steps, log_rate, skip_gain, initial, lens):
    tokens, heads, hdim = xval.shape
    nblk = tokens // BLOCK_LEN
    logd = -(steps * jnp.exp(log_rate)[:, None]).reshape(heads, nblk, BLOCK_LEN)
    cums = jnp.cumsum(logd, axis=2)
    dtc = steps.reshape(heads, nblk, BLOCK_LEN)
    xc = xval.reshape(nblk, BLOCK_LEN, heads, hdim)
    bc = bval.reshape(nblk, BLOCK_LEN, STATE)
    cc = cval.reshape(nblk, BLOCK_LEN, STATE)
    gram = jnp.einsum("ktn,ksn->kts", cc, bc, preferred_element_type=jnp.float32)
    rows = lax.broadcasted_iota(jnp.int32, (BLOCK_LEN, BLOCK_LEN), 0)
    cols = lax.broadcasted_iota(jnp.int32, (BLOCK_LEN, BLOCK_LEN), 1)
    lower = cols <= rows
    gap = jnp.where(lower, cums[:, :, :, None] - cums[:, :, None, :], 0.0)
    weights = jnp.where(lower, jnp.exp(gap) * gram[None] * dtc[:, :, None, :], 0.0).astype(
        jnp.bfloat16
    )
    inner = jnp.einsum("hkts,kshp->kthp", weights, xc, preferred_element_type=jnp.float32)
    tail = jnp.exp(cums[:, :, -1:] - cums) * dtc
    scaled = (xc * jnp.transpose(tail, (1, 2, 0))[..., None]).astype(jnp.bfloat16)
    growth = jnp.einsum("kshp,ksn->khpn", scaled, bc, preferred_element_type=jnp.float32)
    fade = jnp.transpose(jnp.exp(cums[:, :, -1]), (1, 0))
    ends = jnp.cumsum(lens)
    firsts = ends - lens
    index = lax.broadcasted_iota(jnp.int32, (nblk, lens.shape[0]), 0)
    owner_req = jnp.sum(jnp.where(ends[None, :] <= index, 1, 0), axis=1).astype(jnp.int32)
    begins = jnp.any(firsts[None, :] == index, axis=1)

    def advance(carry, item):
        start, which, decay, add = item
        entry = jnp.where(start, initial[which], carry)
        leave = decay[:, None, None] * entry + add
        return (leave, (entry, leave))

    zero = jnp.zeros(initial.shape[1:], jnp.float32)
    _, (entering, leaving) = lax.scan(advance, zero, (begins, owner_req, fade, growth))
    outer = jnp.einsum("ktn,khpn->kthp", cc.astype(jnp.float32), entering, precision=HIGH)
    outer = outer * jnp.exp(jnp.transpose(cums, (1, 2, 0)))[..., None]
    total = inner + outer + skip_gain[None, None, :, None] * xc.astype(jnp.float32)
    finals = jnp.take(leaving, ends - 1, axis=0)
    return (total.reshape(tokens, heads * hdim), finals)


def valve_coefficients(values, gate):
    gated = values * jax.nn.silu(gate.astype(jnp.float32))
    return (gated, jnp.sum(gated * gated, axis=-1))


def finish(gated, totals, gain):
    mean = totals / D_INNER
    return (gated * lax.rsqrt(mean + 1e-05)[..., None] * gain).astype(jnp.bfloat16)


def on_device(
    features,
    gate_input,
    input_map,
    output_map,
    head_step_sizes,
    log_rate,
    skip_gain,
    norm_gain,
    cache_states,
    hit_owner,
    hit_slot,
    suffix_blocks,
    dec_features,
    dec_gate,
    dec_input_map,
    dec_output_map,
    dec_step_size,
):
    owner_count = lax.axis_size("req")
    heads = head_step_sizes.shape[0]
    tokens = features.shape[0]
    requests = hit_slot.shape[0]
    flat = cache_states.shape[2]
    group = lax.axis_index("samp") * heads // (HEADS // GROUPS)
    owners = hit_owner[:, 0]
    ranks = owner_ranks(owners)
    wanted = owners * CAP + ranks
    table = slot_table(owners, ranks, hit_slot, owner_count)
    rows = jnp.take(
        cache_states, lax.all_to_all(table, "req", split_axis=0, concat_axis=0, tiled=True), axis=0
    )
    arrived = lax.all_to_all(rows, "req", split_axis=0, concat_axis=0, tiled=True)
    arrived = arrived.reshape(owner_count * CAP, heads, flat)
    initial = (
        jnp.take(arrived, wanted, axis=0)
        .astype(jnp.float32)
        .reshape(requests, heads, HEAD_DIM, STATE)
    )
    b_rows = lax.dynamic_slice_in_dim(input_map, group * STATE, STATE, 1)
    c_rows = lax.dynamic_slice_in_dim(output_map, group * STATE, STATE, 1)
    values, finals = prefill(
        features.reshape(tokens, heads, HEAD_DIM),
        b_rows,
        c_rows,
        head_step_sizes,
        log_rate,
        skip_gain,
        initial,
        suffix_blocks[0],
    )
    gated_pre, part_pre = valve_coefficients(values, gate_input)
    totals_pre = lax.psum(part_pre, "samp")
    prefill_out = finish(gated_pre, totals_pre, norm_gain)
    samples = dec_features.shape[1]
    steps_n = dec_features.shape[2]
    xd = dec_features.reshape(requests, samples, steps_n, heads, HEAD_DIM).astype(jnp.float32)
    bvals = lax.dynamic_slice_in_dim(dec_input_map, group * STATE, STATE, 3).astype(jnp.float32)
    cvals = lax.dynamic_slice_in_dim(dec_output_map, group * STATE, STATE, 3).astype(jnp.float32)
    dt_t = jnp.transpose(dec_step_size, (1, 2, 3, 0))
    keep_t = jnp.exp(-dt_t * jnp.exp(log_rate))
    state = jnp.broadcast_to(finals[:, None], (requests, samples) + finals.shape[1:])
    outs = []
    for j in range(STEPS):
        push = (dt_t[:, :, j][..., None] * xd[:, :, j])[..., None] * bvals[:, :, j][
            :, :, None, None, :
        ]
        state = keep_t[:, :, j][..., None, None] * state + push
        outs.append(jnp.einsum("rshpn,rsn->rshp", state, cvals[:, :, j], precision=HIGH))
    core = jnp.stack(outs, axis=2)
    dec_values = (core + skip_gain[:, None] * xd).reshape(
        requests, samples, steps_n, heads * HEAD_DIM
    )
    gated_dec, part_dec = valve_coefficients(dec_values, dec_gate)
    totals_dec = lax.psum(part_dec, "samp")
    decode_out = finish(gated_dec, totals_dec, norm_gain)
    return (prefill_out, decode_out)


def solution(mesh):
    return jax.shard_map(
        on_device,
        mesh=mesh,
        in_specs=(
            P("req", "samp"),
            P("req", "samp"),
            P("req", None),
            P("req", None),
            P("samp", "req"),
            P("samp"),
            P("samp"),
            P("samp"),
            P("req", "samp", None),
            P("req", None),
            P("req"),
            P("req", None),
            P("req", None, None, "samp"),
            P("req", None, None, "samp"),
            P("req", None, None, None),
            P("req", None, None, None),
            P("samp", "req", None, None),
        ),
        out_specs=(P("req", "samp"), P("req", None, None, "samp")),
        check_vma=False,
    )
```

profile of v0, /device:TPU:0, one launch (start us, length us, event | category | flops | bytes accessed | tf_op | source)
XLA Modules:
  0.0 630.4 jit_solution(322064329101228794)
XLA Ops:
  4.6 12.7 %all_to_all.20 = s32[32,1,2]{2,1,0:T(1,128)S(1)} all-to-all(s32[32,1,2]{2,1,0:T(1,128)S(1)} %bitcast.141), channel_id=1, replica_groups=mesh['req'=32,'samp'=8] {'req'}, dimensions={0} | all-to-all | bytes 512 | tf_op jit(solution)/shard_map/all_to_all | solution.py:117
  17.7 24.7 %gather_fusion = bf16[64,14,4096]{2,0,1:T(8,128)(2,1)} fusion(bf16[16,14,4096]{2,0,1:T(8,128)(2,1)S(1)} %copy-done, s32[1024]{0:T(1024)S(1)} %pad_clamp_fusion.2), kind=kCustom, calls=%fused_computation | custom fusion | bytes 14680320 | tf_op jit(solution)/shard_map/jit(_take)/gather | solution.py:116
  42.4 12.5 %reshape.153 = bf16[32,2,14,4096]{3,1,0,2:T(2,128)(2,1)} reshape(bf16[64,14,4096]{2,0,1:T(8,128)(2,1)} %gather_fusion) | data formatting | bytes 14680064 | tf_op jit(solution)/shard_map/jit(_take)/gather | solution.py:116
  54.9 9.8 %broadcast_select_fusion = bf16[32,2,14,4096]{3,1,2,0:T(2,128)(2,1)} fusion(pred[32,2]{1,0:T(8,128)(4,1)S(1)} %copy.149, bf16[32,2,14,4096]{3,1,0,2:T(2,128)(2,1)} %reshape.153), kind=kLoop, calls=%fused_computation.26 | loop fusion | flops 3670016 | bytes 14680128 | tf_op jit(solution)/shard_map/jit(_take)/select_n | solution.py:116
  64.7 5.5 all-to-all-start.1
  71.2 3.1 reduce_window_sum.18
  75.5 8.9 %reshape.183 = bf16[24,64,14,64]{3,2,1,0:T(8,128)(2,1)} reshape(bf16[1536,896]{1,0:T(8,128)(2,1)} %param.19) | data formatting | bytes 5505024 | tf_op jit(solution)/shard_map/reshape;reshape | solution.py:40
  87.7 4.5 copy.162
  96.5 3.1 fusion.36
  99.6 10.8 %fusion.24 = f32[24,14,64,64]{3,2,1,0:T(8,128)} fusion(bf16[24,64,64,1]{2,1,3,0:T(8,128)(2,1)S(1)} %bitcast.133, f32[24,64,14]{1,2,0:T(8,128)S(1)} %copy.156, bf16[24,64,14,64]{3,2,1,0:T(8,128)(2,1)} %reshape.183), kind=kOutput, calls=%fused_computation.40 | convolution fusion | flops 180289536 | bytes 8540160 | tf_op jit(solution)/shard_map/kshp,ksn->khpn/dot_general | solution.py:54
  110.4 7.6 %fusion.19 = f32[24,14,64,64]{3,2,1,0:T(8,128)} fusion(f32[14,24,64]{2,0,1:T(8,128)S(1)} %copy-done.11, f32[24,64,64]{2,1,0:T(8,128)S(1)} %fusion.54, f32[14,24,64]{2,0,1:T(8,128)S(1)} %copy.141, pred[64,64]{1,0:T(8,128)(4,1)S(1)} %iota_compare_fusion, bf16[24,64,14,64]{3,2,1,0:T(8,128)(2,1)S(1)} %bitcast.128), kind=kOutput, calls=%fused_computation.35 | convolution fusion | flops 184418304 | bytes 8826880 | tf_op jit(solution)/shard_map/hkts,kshp->kthp/dot_general | solution.py:51
  117.9 44.5 %all-to-all-done.1 = bf16[32,2,14,4096]{3,1,2,0:T(2,128)(2,1)} async-done(((bf16[32,2,14,4096]{3,1,2,0:T(2,128)(2,1)}), bf16[32,2,14,4096]{3,1,2,0:T(2,128)(2,1)}, u32[]{:S(2)}, u32[]{:S(2)}) %all-to-all-start.1) | async-done | bytes 7340064 | tf_op jit(solution)/shard_map/all_to_all | solution.py:119
  162.5 12.5 %copy.153 = bf16[32,2,14,4096]{3,2,1,0:T(8,128)(2,1)} copy(bf16[32,2,14,4096]{3,1,2,0:T(2,128)(2,1)} %all-to-all-done.1) | data formatting | bytes 14680064 | tf_op jit(solution)/shard_map/all_to_all | solution.py:119
  175.0 5.5 gather_fusion.1
  180.4 3.8 copy.154
  184.3 6.3 %gather.16 = bf16[16,14,64,64]{3,2,0,1:T(8,128)(2,1)} reshape(bf16[16,14,4096]{2,0,1:T(8,128)(2,1)} %copy.154) | data formatting | bytes 3670016 | tf_op jit(solution)/shard_map/jit(_take)/gather | solution.py:122
  190.6 5.6 select_convert_fusion.2
  196.2 142.7 %while.15 = (s32[]{:T(128)}, f32[14,64,64]{2,1,0:T(8,128)S(1)}, f32[24,14,64,64]{3,2,1,0:T(8,128)}, f32[24,14,64,64]{3,2,1,0:T(8,128)}, f32[24,14]{1,0:T(8,128)S...) while((s32[]{:T(128)}, f32[14,64,64]{2,1,0:T(8,128)S(1)}, ...), condition=%wide.region_7.8_spmd.clone, body=%wide.region_6.7_spmd.clone.sunk | while | flops 229382 | bytes 2295139 | solution.py:69
  199.3 2.8 bitcast_dynamic-update-slice_fusion.3
  205.2 2.8 bitcast_dynamic-update-slice_fusion.3
  211.2 2.8 bitcast_dynamic-update-slice_fusion.3
  217.1 2.8 bitcast_dynamic-update-slice_fusion.3
  223.1 2.8 bitcast_dynamic-update-slice_fusion.3
  234.9 2.8 bitcast_dynamic-update-slice_fusion.3
  240.9 2.8 bitcast_dynamic-update-slice_fusion.3
  246.8 2.9 bitcast_dynamic-update-slice_fusion.3
  252.8 2.8 bitcast_dynamic-update-slice_fusion.3
  258.7 2.9 bitcast_dynamic-update-slice_fusion.3
  264.7 2.8 bitcast_dynamic-update-slice_fusion.3
  270.7 2.9 bitcast_dynamic-update-slice_fusion.3
  288.5 2.8 bitcast_dynamic-update-slice_fusion.3
  294.4 2.8 bitcast_dynamic-update-slice_fusion.3
  300.4 2.8 bitcast_dynamic-update-slice_fusion.3
  312.3 2.8 bitcast_dynamic-update-slice_fusion.3
  318.2 2.8 bitcast_dynamic-update-slice_fusion.3
  324.2 2.8 bitcast_dynamic-update-slice_fusion.3
  330.1 2.8 bitcast_dynamic-update-slice_fusion.3
  338.8 8.1 %gather_fusion.2 = f32[16,14,64,64]{3,2,1,0:T(8,128)} fusion(f32[24,14,64,64]{3,2,1,0:T(8,128)} %get-tuple-element.51, s32[1024]{0:T(1024)S(1)} %pad_clamp_fusion), kind=kCustom, calls=%fused_computation.2 | custom fusion | bytes 7340096 | tf_op jit(solution)/shard_map/jit(_take)/gather | solution.py:73
  347.0 5.0 broadcast_select_fusion.1
  352.0 101.7 %fusion.1 = f32[16,8,1,14,64]{4,2,3,1,0:T(1,128)S(1)} fusion(f32[16,8,64]{2,1,0:T(8,128)S(1)} %bitcast.144, f32[16,8,14,64]{3,2,1,0:T(8,128)S(1)} %copy-done.5, f32[16,8,14]{2,1,0:T(8,128)S(1)} %copy.170, f32[16,8,64]{2,1,0:T(8,128)S(1)} %bitcast.142, f32[16,8,14,64]{3,2,1,0:T(8,128)S(1)} %copy-done.4, f32[16,14,64,64]{3,2,1,0:T(8,128)S(1)} %broadcast_select_fusion.1, ...), kind=kOutput, calls=%fused_computation.9 | convolution fusion | flops 132120576 | bytes 5142528 | tf_op jit(solution)/shard_map/rshpn,rsn->rshp/dot_general | solution.py:155
  454.2 80.7 %fusion.5 = f32[16,8,1,14,64]{4,2,3,1,0:T(1,128)S(1)} fusion(f32[16,8,64]{2,1,0:T(8,128)S(1)} %bitcast.143, f32[16,8,14,64]{3,2,1,0:T(8,128)} %get-tuple-element.160, f32[16,14,64,64]{3,2,1,0:T(8,128)} %copy-done.2, f32[16,8,14]{2,1,0:T(8,128)S(1)} %copy.163, bf16[16,8,64,1,1]{2,1,0,3,4:T(8,128)(2,1)S(1)} %copy-done.13), kind=kOutput, calls=%fused_computation.14 | convolution fusion | flops 110100480 | bytes 4643840 | tf_op jit(solution)/shard_map/rshpn,rsn->rshp/dot_general | solution.py:155
  535.3 22.1 %fusion.18 = f32[24,64,14,64]{3,1,2,0:T(8,128)} fusion(f32[24,14,64,64]{3,2,1,0:T(8,128)} %fusion.19, f32[14]{0:T(128)S(1)} %copy-done.18, f32[24,64,14]{1,2,0:T(8,128)S(1)} %copy.160, bf16[24,64,64,1]{2,1,3,0:T(8,128)(2,1)S(1)} %bitcast.135, f32[24,14,64,64]{3,2,1,0:T(8,128)} %get-tuple-element.50, bf16[24,64,14,64]{3,2,1,0:T(8,128)(2,1)} %reshape.183), kind=kOutput, calls=%fused_computation.30 | convolution fusion | flops 1063845888 | bytes 19550264 | tf_op jit(solution)/shard_map/ktn,khpn->kthp/dot_general | solution.py:70
  557.5 12.1 %copy.161 = f32[24,64,14,64]{1,0,3,2:T(8,128)} copy(f32[24,64,14,64]{3,1,2,0:T(8,128)} %fusion.18) | data formatting | bytes 11010048 | tf_op jit(solution)/shard_map/add | solution.py:72
  569.6 9.7 %reshape.150 = f32[1536,896]{0,1:T(8,128)} reshape(f32[24,64,14,64]{1,0,3,2:T(8,128)} %copy.161) | data formatting | bytes 11010048 | tf_op jit(solution)/shard_map/reshape | solution.py:74
  579.3 5.3 multiply_reduce_fusion
  585.0 33.1 %all-reduce = (f32[1536]{0:T(1024)S(1)}, f32[16,8,2]{1,0,2:T(8,128)S(1)}) all-reduce(f32[1536]{0:T(1024)S(1)} %multiply_reduce_fusion, f32[16,8,2]{1,0,2:T(8,128)S(1)} %get-tuple-element.157), channel_id=1, replica_groups=mesh['req'=32,'samp'=8] {'samp'}, use_global_device_ids=true, to_apply=%region_9.10 | all-reduce | flops 1792 | bytes 14336 | tf_op jit(solution)/shard_map/psum | solution.py:139
  619.6 5.8 multiply_convert_fusion
  625.4 4.5 copy.173
  (193 shorter events, 58.8 us)
Async XLA Ops:
  0.6 17.0 %copy-start = (bf16[16,14,4096]{2,0,1:T(8,128)(2,1)S(1)}, bf16[16,14,4096]{2,0,1:T(8,128)(2,1)}, u32[]{:S(2)}) copy-start(bf16[16,14,4096]{2,0,1:T(8,128)(2,1)} %param.27) | copy-start | bytes 5505028
  2.5 1.2 copy-start.21
  64.7 6.2 copy-start.22
  64.7 6.2 copy-start.8
  64.7 97.8 %all-to-all-start.1 = ((bf16[32,2,14,4096]{3,1,2,0:T(2,128)(2,1)}), bf16[32,2,14,4096]{3,1,2,0:T(2,128)(2,1)}, u32[]{:S(2)}, u32[]{:S(2)}) async-start(bf16[32,2,14,4096]{3,1,2,0:T(2,128)(2,1)} %broadcast_select_fusion), calls=%async_computation.1 | async-start | bytes 14680064 | tf_op jit(solution)/shard_map/all_to_all | solution.py:119
  70.2 14.4 %copy-start.6 = (f32[14,16,8,2]{1,3,2,0:T(2,128)S(1)}, f32[14,16,8,2]{1,3,2,0:T(2,128)}, u32[]{:S(2)}) copy-start(f32[14,16,8,2]{1,3,2,0:T(2,128)} %param.35) | copy-start | bytes 43012
  70.2 14.7 %copy-start.3 = (bf16[16,8,2,896]{3,2,1,0:T(2,128)(2,1)S(1)}, bf16[16,8,2,896]{3,2,1,0:T(2,128)(2,1)}, u32[]{:S(2)}) copy-start(bf16[16,8,2,896]{3,2,1,0:T(2,128)(2,1)} %param.31) | copy-start | bytes 1376260
  75.5 12.0 %copy-start.17 = (f32[14]{0:T(128)S(1)}, f32[14]{0:T(128)}, u32[]{:S(2)}) copy-start(f32[14]{0:T(128)} %param.25) | copy-start | bytes 172
  84.4 7.8 %copy-start.16 = (s32[16]{0:T(128)S(1)}, s32[16]{0:T(128)}, u32[]{:S(2)}) copy-start(s32[16]{0:T(128)} %get-tuple-element.172) | copy-start | bytes 196
  84.4 7.8 %copy-start.15 = (s32[16]{0:T(128)S(1)}, s32[16]{0:T(128)}, u32[]{:S(2)}) copy-start(s32[16]{0:T(128)} %get-tuple-element.174) | copy-start | bytes 196
  84.4 7.8 %copy-start.20 = (s32[16]{0:T(128)S(1)}, s32[16]{0:T(128)}, u32[]{:S(2)}) copy-start(s32[16]{0:T(128)} %reduce.1) | copy-start | bytes 196
  84.4 7.9 %copy-start.19 = (s32[1,16]{1,0:T(1,128)S(1)}, s32[1,16]{1,0:T(1,128)}, u32[]{:S(2)}) copy-start(s32[1,16]{1,0:T(1,128)} %param.30) | copy-start | bytes 196
  84.4 8.0 %copy-start.12 = (bf16[16,8,2,128]{3,2,1,0:T(2,128)(2,1)S(1)}, bf16[16,8,2,128]{3,2,1,0:T(2,128)(2,1)}, u32[]{:S(2)}) copy-start(bf16[16,8,2,128]{3,2,1,0:T(2,128)(2,1)} %param.33) | copy-start | bytes 196612
  84.5 8.1 %copy-start.10 = (bf16[16,8,2,128]{3,2,1,0:T(2,128)(2,1)S(1)}, bf16[16,8,2,128]{3,2,1,0:T(2,128)(2,1)}, u32[]{:S(2)}) copy-start(bf16[16,8,2,128]{3,2,1,0:T(2,128)(2,1)} %param.34) | copy-start | bytes 196612
  84.5 10.4 %copy-start.9 = (bf16[1536,128]{1,0:T(8,128)(2,1)S(1)}, bf16[1536,128]{1,0:T(8,128)(2,1)}, u32[]{:S(2)}) copy-start(bf16[1536,128]{1,0:T(8,128)(2,1)} %param.21) | copy-start | bytes 1179652
  96.5 13.9 %slice-start = ((s8[6291456]{0:T(1024)(128)(4,1)}), s8[4194304]{0:T(1024)(128)(4,1)S(1)}, s32[]{:S(2)}) async-start(s8[6291456]{0:T(1024)(128)(4,1)} %bitcast.127), calls=%async_computation.2 | async-start | bytes 8388608
  99.6 10.8 %slice-start.1 = ((s8[6291456]{0:T(1024)(128)(4,1)}), s8[2097152]{0:T(1024)(128)(4,1)S(1)}, s32[]{:S(2)}) async-start(s8[6291456]{0:T(1024)(128)(4,1)} %bitcast.127), calls=%async_computation.3 | async-start | bytes 4194304
  99.6 10.8 %copy-start.11 = (f32[14,24,64]{2,0,1:T(8,128)S(1)}, f32[14,24,64]{2,0,1:T(8,128)}, u32[]{:S(2)}) copy-start(f32[14,24,64]{2,0,1:T(8,128)} %copy.143) | copy-start | bytes 258052
  347.0 5.0 copy-start.4
  347.0 5.0 copy-start.5
  351.9 101.8 %copy-start.2 = (f32[16,14,64,64]{3,2,1,0:T(8,128)}, f32[16,14,64,64]{3,2,1,0:T(8,128)S(1)}, u32[]{:S(2)}) copy-start(f32[16,14,64,64]{3,2,1,0:T(8,128)S(1)} %broadcast_select_fusion.1) | copy-start | bytes 11010052
  352.0 102.2 %copy-start.13 = (bf16[16,8,64,1,1]{2,1,0,3,4:T(8,128)(2,1)S(1)}, bf16[16,8,64,1,1]{2,1,0,3,4:T(8,128)(2,1)}, u32[]{:S(2)}) copy-start(bf16[16,8,64,1,1]{2,1,0,3,4:T(8,128)(2,1)} %get-tuple-element.178) | copy-start | bytes 49156
  454.2 81.2 %copy-start.18 = (f32[14]{0:T(128)S(1)}, f32[14]{0:T(128)}, u32[]{:S(2)}) copy-start(f32[14]{0:T(128)} %param.25) | copy-start | bytes 172
  579.3 5.3 copy-start.7
  579.3 38.9 %copy-start.14 = (f32[896]{0:T(1024)S(1)}, f32[896]{0:T(1024)}, u32[]{:S(2)}) copy-start(f32[896]{0:T(1024)} %param.26) | copy-start | bytes 10756
  619.6 10.3 %copy-start.1 = (bf16[16,14,4096]{2,0,1:T(8,128)(2,1)S(1)}, bf16[16,14,4096]{2,0,1:T(8,128)(2,1)}, u32[]{:S(2)}) copy-start(bf16[16,14,4096]{2,0,1:T(8,128)(2,1)} %param.27) | copy-start | bytes 5505028
where the time goes:
time: 642 us; the launch traced here: 630 us
  matrix products  223 us (35%)
  local copies, waits for them, and re-layouts  151 us (24%)
  other arithmetic  112 us (17%)
  loops' own time  46.7 us (7%)
  blocking collectives  45.9 us (7%)
  waiting for transfers between devices  44.5 us (7%)
    dot_general x2, matrix products, on_device(): jnp.einsum('rshpn,rsn->rshp', state, cvals[:, :, j], precision=HIGH)  182 us
    dynamic_update_slice x24, other arithmetic, prefill(): lax.scan(advance, zero, (begins, owner_req, fade, growth))  67.7 us
    another operation x1, loops' own time, prefill(): lax.scan(advance, zero, (begins, owner_req, fade, growth))  46.7 us
    all_to_all x1, waiting for transfers between devices, on_device(): lax.all_to_all(rows, 'req', split_axis=0, concat_axis=0, tiled=True)  44.5 us
    gather x2, local copies, waits for them, and re-layouts, on_device(): jnp.take(cache_states, lax.all_to_all(table, 'req', split_axis=0, concat_...  37.2 us
    psum x1, blocking collectives, on_device(): totals_pre = lax.psum(part_pre, 'samp')  33.1 us
    dynamic_slice x48, local copies, waits for them, and re-layouts, prefill(): lax.scan(advance, zero, (begins, owner_req, fade, growth))  28.2 us
    dot_general x1, matrix products, prefill(): jnp.einsum('ktn,khpn->kthp', cc.astype(jnp.float32), entering, precision=...  22.1 us
  transfers between devices with their start and end apart: 1, of which 1 were waited for; matrix products, arithmetic and copies ran while one was open for 8% of the time, Pallas kernels for 0%

commit v1 on v0

v1 whole, which is shorter than its diff:
```python
import jax
import jax.numpy as jnp
import ml_dtypes
import numpy as np
from jax import lax
from jax.experimental import pallas as pl
from jax.experimental.pallas import tpu as pltpu
from jax.sharding import PartitionSpec as P

HEADS = 112
HEAD_DIM = 64
STATE = 64
GROUPS = 2
BLOCK_LEN = 64
CAP = 2
STEPS = 2
D_INNER = 7168

LOCAL = 14
WIDTH = LOCAL * HEAD_DIM
REQS = 16
OWNERS = 32
NBLK = 24
TOKS = NBLK * BLOCK_LEN
DEC = 16
ROWS = BLOCK_LEN + DEC
QUARTERS = 4
PIECE = STATE // QUARTERS
TILES = tuple(slice(i, min(i + 256, WIDTH)) for i in range(0, WIDTH, 256))
WIDE = 768
TWO = 2
FOUR = 4
PLACES = 3
SHIFTS = ((0, 1), (0, 3), (1, 0), (3, 0))

F32 = jnp.float32
BF16 = jnp.bfloat16
HIGH = lax.Precision.HIGHEST


def dot(a, b):
    return jnp.dot(a, b, preferred_element_type=F32)


def dot_nt(a, b):
    return lax.dot_general(a, b, (((1,), (1,)), ((), ())), preferred_element_type=F32)


def dot_tn(a, b):
    return lax.dot_general(a, b, (((0,), (0,)), ((), ())), preferred_element_type=F32)


def params(mib):
    return pltpu.CompilerParams(vmem_limit_bytes=mib << 20)


def spread_matrix():
    out = np.zeros((2, 32, REQS, REQS, HEAD_DIM), np.float32)
    for parity in range(2):
        for i in range(32):
            for slot in range(REQS):
                out[parity, i, slot, slot, 2 * i + parity] = 1.0
    return out.reshape(1024, 1024).astype(ml_dtypes.bfloat16)


def shifted(device, q):
    y, x, core = device >> 3, (device >> 1) & 3, device & 1
    step = 1 + 2 * (q & 1)
    dy = jnp.where(q >= 2, step, 0)
    dx = jnp.where(q >= 2, 0, step)
    return (((y + dy) & 3) << 3) + (((x + dx) & 3) << 1) + core


def choices(owner, q):
    return owner, owner ^ 1, shifted(owner, q)


def lightest(load, devices):
    a, b, c = (load[device] for device in devices)
    kind = jnp.where((a <= b) & (a <= c), 0, jnp.where(b <= c, 1, 2))
    device = jnp.where(kind == 0, devices[0], jnp.where(kind == 1, devices[1], devices[2]))
    return kind, device, jnp.minimum(a, jnp.minimum(b, c))


def make_plan(owners, slots, table, loc, load, held, seen, origin, queue, late):
    for device in range(OWNERS):
        load[device] = 0
        for place in range(PLACES):
            table[device, place] = 0
    for n in range(REQS * QUARTERS):
        loc[n] = 0

    def put(ball, kind, device, place):
        request, q = ball & 15, ball >> 4
        held[device * PLACES + place] = ball
        loc[request * QUARTERS + q] = device * PLACES + place
        table[device, place] = (kind << 6) + (q << 4) + slots[request]

    waiting = jnp.int32(0)
    for q in range(QUARTERS):
        for request in range(REQS):
            kind, best, room = lightest(load, choices(owners[request], q))
            fits = room < PLACES

            @pl.when(fits)
            def _():
                put((q << 4) + request, kind, best, room)
                load[best] = room + 1

            @pl.when(jnp.logical_not(fits))
            def _():
                late[waiting] = (q << 4) + request

            waiting = waiting + jnp.where(fits, 0, 1)

    def place_late(n, failed):
        ball = late[n]
        for device in range(OWNERS):
            seen[device] = 0

        def visit(options, source, state):
            tail, found = state
            for kind in range(3):
                device = options[kind]
                fresh = (seen[device] == 0) & (found < 0)

                @pl.when(fresh)
                def _():
                    seen[device] = 1
                    origin[device] = (source << 2) + kind
                    queue[tail] = device

                tail = tail + jnp.where(fresh, 1, 0)
                found = jnp.where(fresh & (load[device] < PLACES), device, found)
            return tail, found

        root = OWNERS * PLACES
        start = visit(choices(owners[ball & 15], ball >> 4), root, (jnp.int32(0), jnp.int32(-1)))

        def search(state):
            head, tail, found = state
            device = queue[head]
            for place in range(PLACES):
                spot = device * PLACES + place
                other = held[spot]
                tail, found = visit(choices(owners[other & 15], other >> 4), spot, (tail, found))
            return head + 1, tail, found

        _, _, found = lax.while_loop(
            lambda state: (state[0] < state[1]) & (state[2] < 0),
            search,
            (jnp.int32(0),) + start,
        )

        @pl.when(found >= 0)
        def _():
            room = load[found]
            load[found] = room + 1

            def back(state):
                device, place = state
                source, kind = origin[device] >> 2, origin[device] & 3
                first = source == root
                moved = jnp.where(first, ball, held[jnp.minimum(source, root - 1)])
                put(moved, kind, device, place)
                above = (source * 43) >> 7
                return jnp.where(first, -1, above), source - above * PLACES

            lax.while_loop(lambda state: state[0] >= 0, back, (found, room))

        return failed | jnp.where(found < 0, 1, 0)

    failed = lax.fori_loop(0, waiting, place_late, jnp.int32(0))
    for device in range(OWNERS):
        table[device, PLACES] = failed


def prepare_kernel(
    owners, slots, far_cache, far_spread,
    table, loc, whole, part0, part1, part2, part3,
    cache, spread, turned, load, held, seen, origin, queue, late, sems,
):
    copies = (
        pltpu.make_async_copy(far_cache, cache, sems.at[0]),
        pltpu.make_async_copy(far_spread, spread, sems.at[1]),
    )
    for copy in copies:
        copy.start()
    make_plan(owners, slots, table, loc, load, held, seen, origin, queue, late)
    for copy in copies:
        copy.wait()
    parts = (part0, part1, part2, part3)
    for head in range(LOCAL):
        for chunk in range(4):
            tiles = [
                cache[head, :, (8 * chunk + i) * 128 : (8 * chunk + i + 1) * 128] for i in range(8)
            ]
            block = jnp.concatenate(tiles, axis=0).T
            for parity in range(2):
                first = parity * 512 + chunk * 128
                turned[head * 64 : head * 64 + 64, first : first + 128] = block[
                    parity * 64 : parity * 64 + 64
                ]
    low = lax.broadcasted_iota(jnp.int32, (64, 128), 1) < 64
    for four in range(4):
        out = dot(turned[...], spread[:, four * 256 : four * 256 + 256])
        for two in range(2):
            for pair in range(LOCAL // 2):
                even = out[pair * 128 : pair * 128 + 64, two * 128 : two * 128 + 128]
                odd = out[pair * 128 + 64 : pair * 128 + 128, two * 128 : two * 128 + 128]
                first = jnp.where(low, even, pltpu.roll(odd, 64, 1)).astype(BF16)
                second = jnp.where(low, pltpu.roll(even, 64, 1), odd).astype(BF16)
                for one, value in ((0, first), (1, second)):
                    slot = four * 4 + two * 2 + one
                    for q in range(QUARTERS):
                        piece = value[q * PIECE : (q + 1) * PIECE]
                        whole[q, slot, :, pair * 128 : pair * 128 + 128] = piece
                        parts[q][slot, :, pair * 128 : pair * 128 + 128] = piece


def prepare(owners, slots, cache):
    smem = pl.BlockSpec(memory_space=pltpu.SMEM)
    vmem = pl.BlockSpec(memory_space=pltpu.VMEM)
    anywhere = pl.BlockSpec(memory_space=pl.ANY)
    piece = jax.ShapeDtypeStruct((REQS, PIECE, WIDTH), BF16)
    return pl.pallas_call(
        prepare_kernel,
        out_shape=[
            jax.ShapeDtypeStruct((OWNERS, 4), jnp.int32),
            jax.ShapeDtypeStruct((REQS * QUARTERS,), jnp.int32),
            jax.ShapeDtypeStruct((QUARTERS, REQS, PIECE, WIDTH), BF16),
        ]
        + [piece] * 4,
        in_specs=[smem, smem, anywhere, anywhere],
        out_specs=[smem] * 2 + [vmem] * 5,
        scratch_shapes=[
            pltpu.VMEM((LOCAL, REQS, HEAD_DIM * STATE), BF16),
            pltpu.VMEM((1024, 1024), BF16),
            pltpu.VMEM((LOCAL * 64, 1024), BF16),
            pltpu.SMEM((OWNERS,), jnp.int32),
            pltpu.SMEM((OWNERS * PLACES,), jnp.int32),
            pltpu.SMEM((OWNERS,), jnp.int32),
            pltpu.SMEM((OWNERS,), jnp.int32),
            pltpu.SMEM((OWNERS,), jnp.int32),
            pltpu.SMEM((REQS * QUARTERS,), jnp.int32),
            pltpu.SemaphoreType.DMA((2,)),
        ],
        compiler_params=params(60),
        name="prepare",
    )(owners, slots, jnp.transpose(cache, (1, 0, 2)), jnp.asarray(spread_matrix()))


def collect_kernel(table, own, peer, near0, near1, near2, near3, out, sem):
    near = (near0, near1, near2, near3)

    def each(device, _):
        for place in range(PLACES):
            code = table[device, place]
            kind, q, slot = code >> 6, (code >> 4) & 3, code & 15
            target = out.at[device * PLACES + place]

            @pl.when(kind == 0)
            def _():
                pltpu.make_async_copy(own.at[q, slot], target, sem).start()

            @pl.when(kind == 1)
            def _():
                pltpu.make_async_copy(peer.at[q, slot], target, sem).start()

            for side in range(QUARTERS):

                @pl.when((kind == 2) & (q == side))
                def _():
                    pltpu.make_async_copy(near[side].at[slot], target, sem).start()

        return 0

    lax.fori_loop(0, OWNERS, each, 0)
    pltpu.make_async_copy(out, out, sem).wait()


def collect(table, own, peer, near):
    vmem = pl.BlockSpec(memory_space=pltpu.VMEM)
    return pl.pallas_call(
        collect_kernel,
        out_shape=jax.ShapeDtypeStruct((OWNERS * PLACES, PIECE, WIDTH), BF16),
        in_specs=[pl.BlockSpec(memory_space=pltpu.SMEM)] + [vmem] * 6,
        out_specs=pl.BlockSpec(memory_space=pl.ANY),
        scratch_shapes=[pltpu.SemaphoreType.DMA],
        compiler_params=params(16),
        name="collect",
    )(table, own, peer, *near)


def silu(value):
    return value / (1.0 + jnp.exp(-value))


def thirds(value):
    high = value.astype(BF16).astype(F32)
    rest = value - high
    mid = rest.astype(BF16).astype(F32)
    return jnp.concatenate([high, mid, rest - mid], axis=0)


def before_kernel(
    req_of, x, z, b, c, dt, rates, skip, dx, dz, db, dc, dd, dprev, expand,
    base, slope, growth, left, fade, columns,
):
    @pl.when(pl.program_id(0) == 0)
    def _():
        columns[...] = jnp.zeros_like(columns)

    rate = jnp.exp(rates[...])
    rows = lax.broadcasted_iota(jnp.int32, (BLOCK_LEN, BLOCK_LEN), 0)
    cols = lax.broadcasted_iota(jnp.int32, (BLOCK_LEN, BLOCK_LEN), 1)
    after = jnp.where(rows > cols, 1.0, 0.0).astype(F32)
    drow = lax.broadcasted_iota(jnp.int32, (DEC, DEC), 0)
    dcol = lax.broadcasted_iota(jnp.int32, (DEC, DEC), 1)
    lane = lax.broadcasted_iota(jnp.int32, (DEC, 8), 1)
    grow = lax.broadcasted_iota(jnp.int32, (ROWS, BLOCK_LEN), 0)
    gcol = lax.broadcasted_iota(jnp.int32, (ROWS, BLOCK_LEN), 1)
    live = (gcol <= grow) | (grow >= BLOCK_LEN)

    for n in range(TWO):
        req = req_of[pl.program_id(0) * TWO + n]
        tokens = slice(n * BLOCK_LEN, (n + 1) * BLOCK_LEN)
        step = dt[n]
        decay = step * rate
        left_over = jnp.dot(decay, after, precision=HIGH, preferred_element_type=F32)
        rise = jnp.exp(left_over)
        tail = jnp.exp(-left_over) * step
        whole_fade = jnp.exp(-jnp.sum(decay, axis=1, keepdims=True))
        both = jnp.concatenate([c[tokens], dc[req]], axis=0)
        cross = dot_nt(db[req], dc[req])
        same = jnp.sum(jnp.where(drow == dcol, cross, 0.0), axis=0, keepdims=True)
        prior = jnp.sum(jnp.where(drow + 1 == dcol, cross, 0.0), axis=0, keepdims=True)
        keep = jnp.exp(-dd[req] * rate)
        keep_all = keep * jnp.exp(-dprev[req] * rate)
        columns[n, :, 0:64] = thirds(rise)
        columns[n, :, 64:128] = thirds(tail)
        columns[n, :, 128:144] = thirds(keep_all)
        columns[n, :, 144:160] = thirds(dd[req] * same + skip[...])
        columns[n, :, 160:176] = thirds(keep * dprev[req] * prior)
        columns[n, :, 176:184] = thirds(
            jnp.where(lane == 0, whole_fade, jnp.where(lane == 1, skip[...], 0.0))
        )
        wide = dot_tn(columns[n, :, 0:192].astype(BF16), expand[...])
        rise_w, tail_w = wide[0:64], wide[64:128]
        keep_w, own_w, prior_w = wide[128:144], wide[144:160], wide[160:176]
        skip_w = wide[177:178]
        fade[n] = wide[176:184]

        xf = x[tokens].astype(F32)
        scaled = (xf * tail_w).astype(BF16)
        gram = jnp.where(live, dot_nt(both, b[tokens]), 0.0)
        high = gram.astype(BF16).astype(F32)
        gram2 = jnp.concatenate([high, gram - high], axis=1).astype(BF16)
        inner = dot(gram2, jnp.concatenate([scaled, scaled], axis=0))
        growth[n] = dot_tn(b[tokens], scaled)
        both32 = both.astype(F32)
        left[n] = jnp.concatenate([both32, both32], axis=1).astype(BF16)

        gate = silu(z[tokens].astype(F32))
        base[n, 0:BLOCK_LEN] = (inner[0:BLOCK_LEN] * rise_w + skip_w * xf) * gate
        slope[n, 0:BLOCK_LEN] = rise_w * gate
        dxf = dx[req].astype(F32)
        dgate = silu(dz[req].astype(F32))
        dy = keep_w * inner[BLOCK_LEN:ROWS] + own_w * dxf + prior_w * pltpu.roll(dxf, 1, 0)
        base[n, BLOCK_LEN:ROWS] = dy * dgate
        slope[n, BLOCK_LEN:ROWS] = keep_w * dgate


def expand_matrix():
    out = np.zeros((3, 16, WIDTH), np.float32)
    for head in range(LOCAL):
        out[:, head, head * HEAD_DIM : (head + 1) * HEAD_DIM] = 1.0
    return out.reshape(48, WIDTH).astype(ml_dtypes.bfloat16)


def before(req_of, x, z, b, c, dt, rates, skip, dx, dz, db, dc, dd, dprev):
    def block(*shape):
        return pl.BlockSpec(shape, lambda i, req: (i,) + (0,) * (len(shape) - 1))

    def fixed(*shape):
        return pl.BlockSpec(shape, lambda i, req: (0,) * len(shape))

    return pl.pallas_call(
        before_kernel,
        grid_spec=pltpu.PrefetchScalarGridSpec(
            num_scalar_prefetch=1,
            grid=(NBLK // TWO,),
            in_specs=[
                block(TWO * BLOCK_LEN, WIDTH),
                block(TWO * BLOCK_LEN, WIDTH),
                block(TWO * BLOCK_LEN, STATE),
                block(TWO * BLOCK_LEN, STATE),
                block(TWO, 16, BLOCK_LEN),
                fixed(16, 1),
                fixed(16, 1),
                fixed(REQS, DEC, WIDTH),
                fixed(REQS, DEC, WIDTH),
                fixed(REQS, DEC, STATE),
                fixed(REQS, DEC, STATE),
                fixed(REQS, 16, DEC),
                fixed(REQS, 16, DEC),
                fixed(48, WIDTH),
            ],
            out_specs=[
                block(TWO, ROWS, WIDTH),
                block(TWO, ROWS, WIDTH),
                block(TWO, STATE, WIDTH),
                block(TWO, ROWS, 2 * STATE),
                block(TWO, 8, WIDTH),
            ],
            scratch_shapes=[pltpu.VMEM((TWO, 48, 256), F32)],
        ),
        out_shape=[
            jax.ShapeDtypeStruct((NBLK, ROWS, WIDTH), F32),
            jax.ShapeDtypeStruct((NBLK, ROWS, WIDTH), F32),
            jax.ShapeDtypeStruct((NBLK, STATE, WIDTH), F32),
            jax.ShapeDtypeStruct((NBLK, ROWS, 2 * STATE), BF16),
            jax.ShapeDtypeStruct((NBLK, 8, WIDTH), F32),
        ],
        compiler_params=params(60),
        cost_estimate=pl.CostEstimate(
            flops=NBLK * 2 * 500 * 128 * WIDTH, bytes_accessed=32 << 20, transcendentals=3 << 20
        ),
        name="before",
    )(req_of, x, z, b, c, dt, rates, skip, dx, dz, db, dc, dd, dprev, jnp.asarray(expand_matrix()))


def through_kernel(
    req_of, begins, loc, short, pieces, instead, base, slope, growth, left, fade,
    values, sampled_values, spread, state, first, sums, sem,
):
    step = pl.program_id(0)

    @pl.when(step == 0)
    def _():
        state[...] = jnp.zeros_like(state)

        @pl.when(short[0] == 0)
        def _():
            for n in range(REQS * QUARTERS):
                pltpu.make_async_copy(pieces.at[loc[n]], first.at[n], sem).start()

        @pl.when(short[0] != 0)
        def _():
            for n in range(REQS * QUARTERS):
                pltpu.make_async_copy(instead.at[n], first.at[n], sem).start()

        pltpu.make_async_copy(first, first, sem).wait()

    lane = lax.broadcasted_iota(jnp.int32, (1, 128), 1)
    parts = [jnp.zeros((ROWS, 128), F32)] * FOUR
    for lanes in TILES:
        now = state[:, lanes]
        width = lanes.stop - lanes.start
        for n in range(FOUR):
            k = step * FOUR + n
            req = req_of[k]
            start = first[pl.ds(req * QUARTERS, QUARTERS), :, lanes]
            start = start.reshape(STATE, width).astype(F32)
            faded = jnp.where(begins[k] == 1, start, now) * fade[n, 0:1, lanes]
            high = faded.astype(BF16)
            low = (faded - high.astype(F32)).astype(BF16)
            out = dot(left[n], jnp.concatenate([high, low], axis=0))
            now = faded + growth[n, :, lanes]
            value = base[n, :, lanes] + slope[n, :, lanes] * out
            values[n * BLOCK_LEN : (n + 1) * BLOCK_LEN, lanes] = value[0:BLOCK_LEN]
            sampled_values[pl.ds(pl.multiple_of(req * DEC, DEC), DEC), lanes] = value[
                BLOCK_LEN:ROWS
            ]
            square = value * value
            for tile in range(0, width, 128):
                parts[n] = parts[n] + square[:, tile : tile + 128]
        state[:, lanes] = now
    for n in range(FOUR):
        req = req_of[step * FOUR + n]
        total = jnp.sum(parts[n].T, axis=0, keepdims=True)
        tokens = jnp.concatenate([total[:, 0:BLOCK_LEN]] * 2, axis=1)
        row = step * (FOUR // 2) + n // 2
        sums[pl.ds(row, 1)] = jnp.where(lane >> 6 == n % 2, tokens, sums[pl.ds(row, 1)])
        sampled = jnp.concatenate([total[:, BLOCK_LEN:ROWS]] * 8, axis=1)
        row = NBLK // 2 + (req >> 3)
        sums[pl.ds(row, 1)] = jnp.where(lane >> 4 == (req & 7), sampled, sums[pl.ds(row, 1)])

    @pl.when(step == NBLK // FOUR - 1)
    def _():
        for device in range(8):
            spread[device] = sums[...]


def through(req_of, begins, loc, short, pieces, instead, base, slope, growth, left, fade):
    def block(*shape):
        return pl.BlockSpec(shape, lambda i, *_: (i,) + (0,) * (len(shape) - 1))

    def fixed(*shape):
        return pl.BlockSpec(shape, lambda i, *_: (0,) * len(shape))

    anywhere = pl.BlockSpec(memory_space=pl.ANY)
    return pl.pallas_call(
        through_kernel,
        grid_spec=pltpu.PrefetchScalarGridSpec(
            num_scalar_prefetch=4,
            grid=(NBLK // FOUR,),
            in_specs=[
                anywhere,
                anywhere,
                block(FOUR, ROWS, WIDTH),
                block(FOUR, ROWS, WIDTH),
                block(FOUR, STATE, WIDTH),
                block(FOUR, ROWS, 2 * STATE),
                block(FOUR, 8, WIDTH),
            ],
            out_specs=[
                block(FOUR * BLOCK_LEN, WIDTH),
                fixed(REQS * DEC, WIDTH),
                fixed(8, NBLK // 2 + 2, 128),
            ],
            scratch_shapes=[
                pltpu.VMEM((STATE, WIDTH), F32),
                pltpu.VMEM((REQS * QUARTERS, PIECE, WIDTH), BF16),
                pltpu.VMEM((NBLK // 2 + 2, 128), F32),
                pltpu.SemaphoreType.DMA,
            ],
        ),
        out_shape=[
            jax.ShapeDtypeStruct((TOKS, WIDTH), F32),
            jax.ShapeDtypeStruct((REQS * DEC, WIDTH), F32),
            jax.ShapeDtypeStruct((8, NBLK // 2 + 2, 128), F32),
        ],
        compiler_params=params(62),
        name="through",
    )(req_of, begins, loc, short, pieces, instead, base, slope, growth, left, fade)


def finish_kernel(sums, values, sampled_values, gain, out, dec):
    i = pl.program_id(0)
    last = TOKS // WIDE - 1

    def put(total, source, target):
        scale = lax.rsqrt(total / D_INNER + 1e-05)
        for part in range(source.shape[0] // 128):
            rows = slice(part * 128, part * 128 + 128)
            wide = jnp.broadcast_to(scale[part : part + 1], (128, 128)).T
            for tile in range(WIDTH // 128):
                lanes = slice(tile * 128, (tile + 1) * 128)
                target(rows, lanes, source[rows, lanes] * wide * gain[:, lanes])

    def token(rows, lanes, value):
        out[rows, lanes] = value.astype(BF16)

    def sample(rows, lanes, value):
        first = rows.start // DEC
        dec[first : first + 8, :, :, lanes] = value.reshape(8, 8, 2, 128).astype(BF16)

    for step in range(last + 1):

        @pl.when(i == step)
        def _():
            first = step * WIDE // 128
            put(jnp.sum(sums[:, first : first + WIDE // 128], axis=0), values, token)

    @pl.when(i == last + 1)
    def _():
        put(jnp.sum(sums[:, TOKS // 128 :], axis=0), sampled_values, sample)


def finish(sums, values, sampled_values, gain):
    last = TOKS // WIDE - 1
    return pl.pallas_call(
        finish_kernel,
        grid=(last + 2,),
        in_specs=[
            pl.BlockSpec((8, NBLK // 2 + 2, 128), lambda i: (0, 0, 0)),
            pl.BlockSpec((WIDE, WIDTH), lambda i: (jnp.minimum(i, last), 0)),
            pl.BlockSpec((REQS * DEC, WIDTH), lambda i: (0, 0)),
            pl.BlockSpec((1, WIDTH), lambda i: (0, 0)),
        ],
        out_specs=[
            pl.BlockSpec((WIDE, WIDTH), lambda i: (jnp.minimum(i, last), 0)),
            pl.BlockSpec((REQS, 8, 2, WIDTH), lambda i: (0, 0, 0, 0)),
        ],
        out_shape=[
            jax.ShapeDtypeStruct((TOKS, WIDTH), BF16),
            jax.ShapeDtypeStruct((REQS, 8, 2, WIDTH), BF16),
        ],
        compiler_params=params(60),
        name="finish",
    )(sums, values, sampled_values, gain)


def owner_ranks(owners):
    count = owners.shape[-1]
    same = owners[..., :, None] == owners[..., None, :]
    rows = lax.broadcasted_iota(jnp.int32, (count, count), 0)
    cols = lax.broadcasted_iota(jnp.int32, (count, count), 1)
    return jnp.sum(jnp.where(same & (cols < rows), 1, 0), axis=-1).astype(jnp.int32)


def fetch_all(owners, slots, own):
    wanted = owners * CAP + owner_ranks(owners)
    grid = lax.broadcasted_iota(jnp.int32, (1, OWNERS * CAP), 1)
    table = jnp.sum(jnp.where(wanted[:, None] == grid, slots[:, None], 0), axis=0)
    table = lax.all_to_all(
        table.reshape(OWNERS, CAP), "req", split_axis=0, concat_axis=0, tiled=True
    ).reshape(-1)
    quarter = lax.broadcasted_iota(jnp.int32, (1, QUARTERS), 1)
    rows = jnp.take(own, table[:, None] + REQS * quarter, axis=0)
    arrived = lax.all_to_all(rows, "req", split_axis=0, concat_axis=0, tiled=True)
    arrived = arrived.reshape(OWNERS * CAP * QUARTERS, PIECE, WIDTH)
    mine = jnp.take(arrived, (wanted[:, None] * QUARTERS + quarter).reshape(-1), axis=0)
    rest = jnp.zeros((OWNERS * PLACES - REQS * QUARTERS, PIECE, WIDTH), BF16)
    return jnp.concatenate([mine, rest], axis=0)


def moves(dy, dx, dcore):
    return [
        (
            (y * 4 + x) * 2 + core,
            (((y + dy) % 4) * 4 + (x + dx) % 4) * 2 + (core + dcore) % 2,
        )
        for y in range(4)
        for x in range(4)
        for core in range(2)
    ]


def exchange(value, axis):
    return lax.all_to_all(value, axis, split_axis=0, concat_axis=0, tiled=True)


def on_device(
    features,
    gate_input,
    input_map,
    output_map,
    head_step_sizes,
    log_rate,
    skip_gain,
    norm_gain,
    cache_states,
    hit_owner,
    hit_slot,
    suffix_blocks,
    dec_features,
    dec_gate,
    dec_input_map,
    dec_output_map,
    dec_step_size,
):
    group = lax.axis_index("samp") * LOCAL // (HEADS // GROUPS)
    owners = hit_owner[:, 0]

    table, loc, own, *quarters = prepare(owners, hit_slot, cache_states)
    near = [
        lax.ppermute(quarters[q], "req", moves(*SHIFTS[q], 0)) for q in range(QUARTERS)
    ]
    peer = lax.ppermute(own, "req", moves(0, 0, 1))
    asked = exchange(table, "req")
    short = jnp.max(asked[:, PLACES])
    sent = lax.cond(
        short > 0,
        lambda: fetch_all(owners, hit_slot, own.reshape(QUARTERS * REQS, PIECE, WIDTH)),
        lambda: collect(asked, own, peer, near),
    )
    pieces = exchange(sent, "req")

    lens = suffix_blocks[0]
    ends = jnp.cumsum(lens)
    index = lax.broadcasted_iota(jnp.int32, (NBLK, REQS), 0)
    req_of = jnp.sum(jnp.where(ends[None, :] <= index, 1, 0), axis=1).astype(jnp.int32)
    begins = jnp.any((ends - lens)[None, :] == index, axis=1).astype(jnp.int32)
    b_rows = lax.dynamic_slice_in_dim(input_map, group * STATE, STATE, 1)
    c_rows = lax.dynamic_slice_in_dim(output_map, group * STATE, STATE, 1)
    db = lax.dynamic_slice_in_dim(dec_input_map, group * STATE, STATE, 3)
    dc = lax.dynamic_slice_in_dim(dec_output_map, group * STATE, STATE, 3)
    pad = ((0, 0), (0, 16 - LOCAL), (0, 0))
    dt = jnp.transpose(head_step_sizes.reshape(LOCAL, NBLK, BLOCK_LEN), (1, 0, 2))
    dd = jnp.transpose(dec_step_size, (1, 0, 2, 3))
    dprev = jnp.concatenate([jnp.zeros_like(dd[..., :1]), dd[..., :1]], axis=3)
    tall = ((0, 16 - LOCAL), (0, 0))
    base, slope, growth, left, fade = before(
        req_of,
        features,
        gate_input,
        b_rows,
        c_rows,
        jnp.pad(dt, pad),
        jnp.pad(log_rate[:, None], tall),
        jnp.pad(skip_gain[:, None], tall),
        dec_features.reshape(REQS, DEC, WIDTH),
        dec_gate.reshape(REQS, DEC, WIDTH),
        db.reshape(REQS, DEC, STATE),
        dc.reshape(REQS, DEC, STATE),
        jnp.pad(dd.reshape(REQS, LOCAL, DEC), pad),
        jnp.pad(dprev.reshape(REQS, LOCAL, DEC), pad),
    )

    values, sampled_values, sums = through(
        req_of, begins, loc, short[None], pieces, sent, base, slope, growth, left, fade
    )
    totals = exchange(sums, "samp")
    prefill_out, decode_out = finish(totals, values, sampled_values, norm_gain[None])
    return (prefill_out, decode_out)


def solution(mesh):
    return jax.shard_map(
        on_device,
        mesh=mesh,
        in_specs=(
            P("req", "samp"),
            P("req", "samp"),
            P("req", None),
            P("req", None),
            P("samp", "req"),
            P("samp"),
            P("samp"),
            P("samp"),
            P("req", "samp", None),
            P("req", None),
            P("req"),
            P("req", None),
            P("req", None, None, "samp"),
            P("req", None, None, "samp"),
            P("req", None, None, None),
            P("req", None, None, None),
            P("samp", "req", None, None),
        ),
        out_specs=(P("req", "samp"), P("req", None, None, "samp")),
        check_vma=False,
    )
```

time: 642 us -> 110 us (0.17); the launches traced: 630 us -> 109 us
  matrix products: 223 us -> 0 us
  local copies, waits for them, and re-layouts: 151 us -> 9.33 us
  other arithmetic: 112 us -> 2.1 us
  Pallas kernels: 0 us -> 53.2 us
  loops' own time: 46.7 us -> 0.02 us
  blocking collectives: 45.9 us -> 0 us
  waiting for transfers between devices: 44.5 us -> 19.5 us
  starting transfers between devices: 5.48 us -> 23.4 us
    dot_general x6 -> x0, matrix products: 223 us -> none  [the longest x2 182 us: on_device(): jnp.einsum('rshpn,rsn->rshp', state, cvals[:, :, j], precision=HIGH)]
    dynamic_update_slice x24 -> x0, other arithmetic: 67.7 us -> none  [prefill(): lax.scan(advance, zero, (begins, owner_req, fade, growth))]
    gather x6 -> x0, local copies, waits for them, and re-layouts: 60.9 us -> none  [the longest x2 37.2 us: on_device(): jnp.take(cache_states, lax.all_to_all(table, 'req', split_axis=0, concat_...]
    pallas_call x0 -> x5, Pallas kernels: none -> 53.2 us  [the longest x1 23.5 us: before(): pl.pallas_call(before_kernel, grid_spec=pltpu.PrefetchScalarGridSpec(num_...]
    another operation x1, loops' own time: 46.7 us -> 0.02 us  [on_device(): lax.cond(short > 0, lambda: fetch_all(owners, hit_slot, own.reshape(QUART...]
    psum x1 -> x0, blocking collectives: 33.1 us -> none  [on_device(): totals_pre = lax.psum(part_pre, 'samp')]
    dynamic_slice x49 -> x2, local copies, waits for them, and re-layouts: 29.4 us -> 2.04 us  [the longest x1 1.17 us: on_device(): c_rows = lax.dynamic_slice_in_dim(output_map, group * STATE, STATE, 1)]
    all_to_all x1 -> x3, waiting for transfers between devices: 44.5 us -> 19.5 us  [exchange(): return lax.all_to_all(value, axis, split_axis=0, concat_axis=0, tiled=True)]
  transfers between devices with their start and end apart: 1 -> 8, of which waited for: 1 -> 3; matrix products, arithmetic and copies ran while one was open for 8% -> 10% of each run, Pallas kernels for 0% -> 21%
where the time goes in v1:
time: 110 us; the launch traced here: 109 us
  Pallas kernels  53.2 us (48%)
  starting transfers between devices  23.4 us (21%)
  waiting for transfers between devices  19.5 us (18%)
  local copies, waits for them, and re-layouts  9.33 us (8%)
  other arithmetic  2.1 us (2%)
  between operations  1.56 us (1%)
    pallas_call x1, Pallas kernels, before(): pl.pallas_call(before_kernel, grid_spec=pltpu.PrefetchScalarGridSpec(num_...  23.5 us
    all_to_all x3, waiting for transfers between devices, exchange(): return lax.all_to_all(value, axis, split_axis=0, concat_axis=0, tiled=True)  19.5 us
    all_to_all x3, starting transfers between devices, exchange(): return lax.all_to_all(value, axis, split_axis=0, concat_axis=0, tiled=True)  16.8 us
    pallas_call x1, Pallas kernels, through(): pl.pallas_call(through_kernel, grid_spec=pltpu.PrefetchScalarGridSpec(num...  14.4 us
    pallas_call x1, Pallas kernels, prepare(): pl.pallas_call(prepare_kernel, out_shape=[jax.ShapeDtypeStruct((OWNERS, 4...  6.6 us
    ppermute x4, starting transfers between devices, on_device(): lax.ppermute(quarters[q], 'req', moves(*SHIFTS[q], 0))  6.54 us
    pallas_call x1, Pallas kernels, finish(): pl.pallas_call(finish_kernel, grid=(last + 2,), in_specs=[pl.BlockSpec((8...  5.17 us
    pallas_call x1, Pallas kernels, collect(): pl.pallas_call(collect_kernel, out_shape=jax.ShapeDtypeStruct((OWNERS * P...  3.55 us
  transfers between devices with their start and end apart: 8, of which 3 were waited for; matrix products, arithmetic and copies ran while one was open for 10% of the time, Pallas kernels for 21%

profile of v1, /device:TPU:0, one launch (start us, length us, event | category | flops | bytes accessed | tf_op | source)
XLA Modules:
  0.0 109.1 jit_solution(10948126040405131460)
XLA Ops:
  0.7 6.6 %prepare.1 = (s32[32,4]{1,0:T(8,128)}, s32[64]{0:T(128)}, bf16[4,16,16,896]{3,2,1,0:T(8,128)(2,1)S(1)}, bf16[16,16,896]{2,1,0:T(8,128)(2,1)}, bf16[16,16,896]{2,...) custom-call(s32[16]{0:T(128)} %bitcast.46, s32[16]{0:T(128)} %slots.1, ...), custom_call_target="tpu_custom_call" | custom-call | tf_op jit(solution)/shard_map/prepare/pallas_call | solution.py:226
  7.3 0.1 collective-permute-start
  7.4 0.1 collective-permute-start.1
  7.5 3.2 %collective-permute-start.2 = (bf16[16,16,896]{2,1,0:T(8,128)(2,1)}, bf16[16,16,896]{2,1,0:T(8,128)(2,1)S(1)}, u32[]{:S(2)}, u32[]{:S(2)}) collective-permute-start(bf16[16,16,896]{2,1,0:T(8,128)(2,1)} %get-tuple-element.57), channel_id=1, source_target_pairs={{0,48},{8,56},{16,0},{24,8},{32,16},{40,24},{48,32},{56,40},{64,11... | collective-permute-start | bytes 1376264 | tf_op jit(solution)/shard_map/ppermute | solution.py:659
  10.7 3.2 %collective-permute-start.4 = (bf16[16,16,896]{2,1,0:T(8,128)(2,1)}, bf16[16,16,896]{2,1,0:T(8,128)(2,1)}, u32[]{:S(2)}, u32[]{:S(2)}) collective-permute-start(bf16[16,16,896]{2,1,0:T(8,128)(2,1)} %get-tuple-element.59), channel_id=1, source_target_pairs={{0,192},{8,200},{16,208},{24,216},{32,224},{40,232},{48,240},{56,2... | collective-permute-start | bytes 1376264 | tf_op jit(solution)/shard_map/ppermute | solution.py:659
  13.9 3.8 %all-to-all-start.2 = ((s32[32,1,4]{2,1,0:T(1,128)}), s32[32,1,4]{2,1,0:T(1,128)S(1)}, u32[]{:S(2)}, u32[]{:S(2)}) async-start(s32[32,1,4]{2,1,0:T(1,128)} %bitcast.43), calls=%async_computation.2 | async-start | bytes 32768 | tf_op jit(solution)/shard_map/all_to_all | solution.py:632
  17.8 7.3 %all-to-all-done.2 = s32[32,1,4]{2,1,0:T(1,128)S(1)} async-done(((s32[32,1,4]{2,1,0:T(1,128)}), s32[32,1,4]{2,1,0:T(1,128)S(1)}, u32[]{:S(2)}, u32[]{:S(2)}) %all-to-all-start.2) | async-done | bytes 544 | tf_op jit(solution)/shard_map/all_to_all | solution.py:632
  25.1 0.1 copy.63
  25.2 0.7 slice_reduce_fusion
  26.5 3.7 %conditional.1 = (bf16[96,16,896]{2,1,0:T(8,128)(2,1)}) conditional(s32[]{:T(128)} %convert_element_type.15, (s32[32,4]{0,1:T(4,128)S(1)}, bf16[4,16,16,896]{3,2,1,0:T(8,128)(2,1)S(1)}, bf16[4,16,16,896]{3,2,1,0:T(8,128)(2,1)}, bf16[16,16,896]{2,1,0:T(8,128)(2,1)S(1)}, bf16[16,16,896]{2,1,0:T(8,128)(2,1)S(1)}, ...), branch_computations={%region_4.5_spmd, %region_5.8_spmd} | conditional | flops 4597348 | bytes 63360840 | solution.py:664
  26.6 0.1 copy.64.table
  26.6 3.6 %collect.1 = bf16[96,16,896]{2,1,0:T(8,128)(2,1)} custom-call(s32[32,4]{1,0:T(8,128)S(1)} %copy.64.table, bf16[4,16,16,896]{3,2,1,0:T(8,128)(2,1)S(1)} %get-tuple-element.26.own, bf16[4,16,16,896]{3,2,1,0:T(8,128)(2,1)} %get-tuple-element.27.peer, bf16[16,16,896]{2,1,0:T(8,128)(2,1)S(1)} %get-tuple-element.28.near0, ...), custom_call_target="tpu_custom_call" | custom-call | tf_op jit(solution)/shard_map/cond/branch_0_fun/collect/pallas_call | solution.py:284
  30.2 0.0 copy-start.12
  30.2 0.0 copy-start.6
  30.2 0.0 copy-start.13
  30.3 0.0 copy-start.1
  30.3 5.2 %all-to-all-start.3 = ((bf16[96,16,896]{2,1,0:T(8,128)(2,1)}), bf16[96,16,896]{2,1,0:T(8,128)(2,1)}, u32[]{:S(2)}, u32[]{:S(2)}) async-start(bf16[96,16,896]{2,1,0:T(8,128)(2,1)} %get-tuple-element.109.instead), calls=%async_computation.3 | async-start | bytes 5505024 | tf_op jit(solution)/shard_map/all_to_all | solution.py:632
  35.4 0.0 copy-start.5
  35.5 0.0 copy-start.7
  35.5 0.0 copy-start.3
  35.5 0.1 copy.60
  35.7 0.1 reduce.2
  35.8 0.1 fusion.5
  35.9 0.6 convert_element_type.14.begins
  36.5 0.1 reshape.177
  36.6 0.1 copy.66
  36.7 0.7 pad.20.dt
  37.4 0.6 pad.21.rates
  38.0 0.1 copy.67
  38.1 0.6 pad.22.skip
  38.7 0.9 reshape.178.dx
  39.6 1.0 reshape.179.dz
  40.6 0.1 copy.68
  40.7 0.7 pad.23.dd
  41.4 0.1 concatenate.6
  41.5 0.1 copy.69
  41.6 0.7 pad.24.dprev
  42.3 0.6 select_reduce_fusion.2.req_of
  42.9 0.9 constant_dynamic-slice_fusion
  43.8 1.2 %constant_dynamic-slice_fusion.2 = (bf16[1536,64]{1,0:T(8,128)(2,1)}, bf16[1536,64]{1,0:T(8,128)(2,1)}) fusion(bf16[1536,128]{1,0:T(8,128)(2,1)S(1)} %copy-done.2, s32[]{:T(128)S(6)} %select_n.65, bf16[1536,128]{1,0:T(8,128)(2,1)S(1)} %copy-done.3), kind=kLoop, calls=%fused_computation.31 | loop fusion | bytes 786436 | tf_op jit(solution)/shard_map/dynamic_slice | solution.py:677
  44.9 23.5 %before.1 = (f32[24,80,896]{2,1,0:T(8,128)}, f32[24,80,896]{2,1,0:T(8,128)}, f32[24,64,896]{2,1,0:T(8,128)}, bf16[24,80,128]{2,1,0:T(8,128)(2,1)}, f32[24,8,896]{2,1,0:T(8,128)}) custom-call(s32[24]{0:T(128)} %select_reduce_fusion.2.req_of, bf16[1536,896]{1,0:T(8,128)(2,1)} %x.15, bf16[1536,896]{1,0:T(8,128)(2,1)} %z.1, ...), custom_call_target="tpu_custom_call" | custom-call | flops 2752512000 | bytes 33554432 | tf_op jit(solution)/shard_map/before/pallas_call | solution.py:388
  68.4 4.3 %all-to-all-done.3.pieces = bf16[96,16,896]{2,1,0:T(8,128)(2,1)} async-done(((bf16[96,16,896]{2,1,0:T(8,128)(2,1)}), bf16[96,16,896]{2,1,0:T(8,128)(2,1)}, u32[]{:S(2)}, u32[]{:S(2)}) %all-to-all-start.3) | async-done | bytes 2752544 | tf_op jit(solution)/shard_map/all_to_all | solution.py:632
  72.7 14.4 %through.1 = (f32[1536,896]{1,0:T(8,128)}, f32[256,896]{1,0:T(8,128)}, f32[8,14,128]{2,1,0:T(8,128)}) custom-call(s32[24]{0:T(128)} %select_reduce_fusion.2.req_of, s32[24]{0:T(128)} %convert_element_type.14.begins, s32[64]{0:T(128)} %get-tuple-element.53.loc, s32[1]{0:T(128)} %bitcast.12.short, bf16[96,16,896]{2,1,0:T(8,128)(2,1)} %all-to-all-done.3.pieces, ...), custom_call_target="tpu_custom_call" | custom-call | tf_op jit(solution)/shard_map/through/pallas_call | solution.py:503
  87.1 7.8 %all-to-all-start.4 = ((f32[8,14,128]{2,1,0:T(8,128)}), f32[8,14,128]{2,1,0:T(8,128)S(1)}, u32[]{:S(2)}, u32[]{:S(2)}) async-start(f32[8,14,128]{2,1,0:T(8,128)} %get-tuple-element.65), calls=%async_computation.4 | async-start | bytes 131072 | tf_op jit(solution)/shard_map/all_to_all | solution.py:632
  94.9 0.6 broadcast_in_dim.71.gain
  95.5 7.8 %all-to-all-done.4.sums = f32[8,14,128]{2,1,0:T(8,128)S(1)} async-done(((f32[8,14,128]{2,1,0:T(8,128)}), f32[8,14,128]{2,1,0:T(8,128)S(1)}, u32[]{:S(2)}, u32[]{:S(2)}) %all-to-all-start.4) | async-done | bytes 57376 | tf_op jit(solution)/shard_map/all_to_all | solution.py:632
  103.3 0.6 copy-done.4
  103.9 5.2 %finish.1 = (bf16[1536,896]{1,0:T(8,128)(2,1)}, bf16[16,8,2,896]{3,2,1,0:T(2,128)(2,1)}) custom-call(f32[8,14,128]{2,1,0:T(8,128)} %copy-done.4, f32[1536,896]{1,0:T(8,128)} %get-tuple-element.66.values, f32[256,896]{1,0:T(8,128)} %get-tuple-element.67.sampled_values, f32[1,896]{1,0:T(1,128)} %broadcast_in_dim.71.gain), custom_call_target="tpu_custom_call" | custom-call | tf_op jit(solution)/shard_map/finish/pallas_call | solution.py:573
  (32 shorter events, 0.2 us)
Async XLA Ops:
  0.6 25.9 %copy-start.10 = (s32[16,1]{0,1:T(1,128)S(1)}, s32[16,1]{0,1:T(1,128)}, u32[]{:S(2)}) copy-start(s32[16,1]{0,1:T(1,128)} %param.30) | copy-start | bytes 196
  0.6 25.9 %copy-start.11 = (s32[16]{0:T(128)S(1)}, s32[16]{0:T(128)}, u32[]{:S(2)}) copy-start(s32[16]{0:T(128)} %slots.1) | copy-start | bytes 196
  7.3 19.3 %collective-permute-start = (bf16[4,16,16,896]{3,2,1,0:T(8,128)(2,1)S(1)}, bf16[4,16,16,896]{3,2,1,0:T(8,128)(2,1)}, u32[]{:S(2)}, u32[]{:S(2)}) collective-permute-start(bf16[4,16,16,896]{3,2,1,0:T(8,128)(2,1)S(1)} %get-tuple-element.55), channel_id=1, source_target_pairs={{0,8},{8,0},{16,24},{24,16},{32,40},{40,32},{48,56},{56,48},{64,72... | collective-permute-start | bytes 5505032 | tf_op jit(solution)/shard_map/ppermute | solution.py:661
  7.4 19.1 %collective-permute-start.1 = (bf16[16,16,896]{2,1,0:T(8,128)(2,1)}, bf16[16,16,896]{2,1,0:T(8,128)(2,1)S(1)}, u32[]{:S(2)}, u32[]{:S(2)}) collective-permute-start(bf16[16,16,896]{2,1,0:T(8,128)(2,1)} %get-tuple-element.56), channel_id=1, source_target_pairs={{0,16},{8,24},{16,32},{24,40},{32,48},{40,56},{48,0},{56,8},{64,80... | collective-permute-start | bytes 1376264 | tf_op jit(solution)/shard_map/ppermute | solution.py:659
  7.5 19.0 %collective-permute-start.2 = (bf16[16,16,896]{2,1,0:T(8,128)(2,1)}, bf16[16,16,896]{2,1,0:T(8,128)(2,1)S(1)}, u32[]{:S(2)}, u32[]{:S(2)}) collective-permute-start(bf16[16,16,896]{2,1,0:T(8,128)(2,1)} %get-tuple-element.57), channel_id=1, source_target_pairs={{0,48},{8,56},{16,0},{24,8},{32,16},{40,24},{48,32},{56,40},{64,11... | collective-permute-start | bytes 1376264 | tf_op jit(solution)/shard_map/ppermute | solution.py:659
  10.7 15.8 %collective-permute-start.3 = (bf16[16,16,896]{2,1,0:T(8,128)(2,1)}, bf16[16,16,896]{2,1,0:T(8,128)(2,1)S(1)}, u32[]{:S(2)}, u32[]{:S(2)}) collective-permute-start(bf16[16,16,896]{2,1,0:T(8,128)(2,1)} %get-tuple-element.58), channel_id=1, source_target_pairs={{0,64},{8,72},{16,80},{24,88},{32,96},{40,104},{48,112},{56,120},{... | collective-permute-start | bytes 1376264 | tf_op jit(solution)/shard_map/ppermute | solution.py:659
  10.7 15.8 %collective-permute-start.4 = (bf16[16,16,896]{2,1,0:T(8,128)(2,1)}, bf16[16,16,896]{2,1,0:T(8,128)(2,1)}, u32[]{:S(2)}, u32[]{:S(2)}) collective-permute-start(bf16[16,16,896]{2,1,0:T(8,128)(2,1)} %get-tuple-element.59), channel_id=1, source_target_pairs={{0,192},{8,200},{16,208},{24,216},{32,224},{40,232},{48,240},{56,2... | collective-permute-start | bytes 1376264 | tf_op jit(solution)/shard_map/ppermute | solution.py:659
  13.9 11.2 %all-to-all-start.2 = ((s32[32,1,4]{2,1,0:T(1,128)}), s32[32,1,4]{2,1,0:T(1,128)S(1)}, u32[]{:S(2)}, u32[]{:S(2)}) async-start(s32[32,1,4]{2,1,0:T(1,128)} %bitcast.43), calls=%async_computation.2 | async-start | bytes 32768 | tf_op jit(solution)/shard_map/all_to_all | solution.py:632
  30.2 5.3 %copy-start.12 = (s32[1,16]{1,0:T(1,128)S(1)}, s32[1,16]{1,0:T(1,128)}, u32[]{:S(2)}) copy-start(s32[1,16]{1,0:T(1,128)} %param.32) | copy-start | bytes 196
  30.2 6.2 %copy-start.6 = (f32[14,1536]{1,0:T(8,128)S(1)}, f32[14,1536]{1,0:T(8,128)}, u32[]{:S(2)}) copy-start(f32[14,1536]{1,0:T(8,128)} %param.25) | copy-start | bytes 258052
  30.2 6.4 %copy-start.13 = (f32[14]{0:T(128)S(1)}, f32[14]{0:T(128)}, u32[]{:S(2)}) copy-start(f32[14]{0:T(128)} %param.26) | copy-start | bytes 172
  30.2 7.8 %copy-start.14 = (f32[14]{0:T(128)S(1)}, f32[14]{0:T(128)}, u32[]{:S(2)}) copy-start(f32[14]{0:T(128)} %param.27) | copy-start | bytes 172
  30.3 8.4 %copy-start = (bf16[16,8,2,896]{3,2,1,0:T(2,128)(2,1)S(1)}, bf16[16,8,2,896]{3,2,1,0:T(2,128)(2,1)}, u32[]{:S(2)}) copy-start(bf16[16,8,2,896]{3,2,1,0:T(2,128)(2,1)} %param.33) | copy-start | bytes 1376260
  30.3 9.4 %copy-start.1 = (bf16[16,8,2,896]{3,2,1,0:T(2,128)(2,1)S(1)}, bf16[16,8,2,896]{3,2,1,0:T(2,128)(2,1)}, u32[]{:S(2)}) copy-start(bf16[16,8,2,896]{3,2,1,0:T(2,128)(2,1)} %param.34) | copy-start | bytes 1376260
  30.3 42.5 %all-to-all-start.3 = ((bf16[96,16,896]{2,1,0:T(8,128)(2,1)}), bf16[96,16,896]{2,1,0:T(8,128)(2,1)}, u32[]{:S(2)}, u32[]{:S(2)}) async-start(bf16[96,16,896]{2,1,0:T(8,128)(2,1)} %get-tuple-element.109.instead), calls=%async_computation.3 | async-start | bytes 5505024 | tf_op jit(solution)/shard_map/all_to_all | solution.py:632
  35.4 5.2 %copy-start.5 = (f32[14,16,8,2]{1,3,2,0:T(2,128)S(1)}, f32[14,16,8,2]{1,3,2,0:T(2,128)}, u32[]{:S(2)}) copy-start(f32[14,16,8,2]{1,3,2,0:T(2,128)} %param.37) | copy-start | bytes 43012
  35.5 7.4 %copy-start.7 = (bf16[16,8,2,128]{3,2,1,0:T(2,128)(2,1)S(1)}, bf16[16,8,2,128]{3,2,1,0:T(2,128)(2,1)}, u32[]{:S(2)}) copy-start(bf16[16,8,2,128]{3,2,1,0:T(2,128)(2,1)} %param.36) | copy-start | bytes 196612
  35.5 7.4 %copy-start.8 = (bf16[16,8,2,128]{3,2,1,0:T(2,128)(2,1)S(1)}, bf16[16,8,2,128]{3,2,1,0:T(2,128)(2,1)}, u32[]{:S(2)}) copy-start(bf16[16,8,2,128]{3,2,1,0:T(2,128)(2,1)} %param.35) | copy-start | bytes 196612
  35.5 8.3 %copy-start.2 = (bf16[1536,128]{1,0:T(8,128)(2,1)S(1)}, bf16[1536,128]{1,0:T(8,128)(2,1)}, u32[]{:S(2)}) copy-start(bf16[1536,128]{1,0:T(8,128)(2,1)} %param.24) | copy-start | bytes 1179652
  35.5 8.3 %copy-start.3 = (bf16[1536,128]{1,0:T(8,128)(2,1)S(1)}, bf16[1536,128]{1,0:T(8,128)(2,1)}, u32[]{:S(2)}) copy-start(bf16[1536,128]{1,0:T(8,128)(2,1)} %param.23) | copy-start | bytes 1179652
  72.7 22.2 %copy-start.9 = (f32[896]{0:T(1024)S(1)}, f32[896]{0:T(1024)}, u32[]{:S(2)}) copy-start(f32[896]{0:T(1024)} %param.28) | copy-start | bytes 10756
  87.1 16.2 %all-to-all-start.4 = ((f32[8,14,128]{2,1,0:T(8,128)}), f32[8,14,128]{2,1,0:T(8,128)S(1)}, u32[]{:S(2)}, u32[]{:S(2)}) async-start(f32[8,14,128]{2,1,0:T(8,128)} %get-tuple-element.65), calls=%async_computation.4 | async-start | bytes 131072 | tf_op jit(solution)/shard_map/all_to_all | solution.py:632
  103.3 0.6 copy-start.4
